TPU v7x, 32 devices: a whole 2x2x4 slice. The times are simulated.
32 devices in a mesh: dp: 2 (over core), seq: 16 (over z, y, x).
Axes of the slice: x: 2, y: 2, z: 4, core: 2. Of those that a mesh axis runs over, the one named last changes fastest.
Arguments:
- y_first: bfloat16 [2, 32, 64, 1152], P('dp', 'seq'), may hold values from -10 to 10
- y_second: bfloat16 [2, 32, 64, 1152], P('dp', 'seq'), may hold values from -10 to 10
- grad_first: bfloat16 [2, 32, 64, 1152], P('dp', 'seq'), may hold values from -6 to 6
- grad_second: bfloat16 [2, 32, 64, 1152], P('dp', 'seq'), may hold values from -6 to 6
- w_qkv_space: bfloat16 [1152, 1728], P('seq', 'dp'), may hold values from -1 to 1
- w_out_space: bfloat16 [576, 1152], P('seq', 'dp'), may hold values from -0.25 to 0.25
- w_qkv_time: bfloat16 [1152, 1728], P('seq', 'dp'), may hold values from -1 to 1
- w_out_time: bfloat16 [576, 1152], P('seq', 'dp'), may hold values from -0.25 to 0.25
Outputs:
- x_first: bfloat16 [2, 32, 64, 1152], P('dp', 'seq')
- x_second: bfloat16 [2, 32, 64, 1152], P('dp', 'seq')
- d_first: bfloat16 [2, 32, 64, 1152], P('dp', 'seq')
- d_second: bfloat16 [2, 32, 64, 1152], P('dp', 'seq')
- grad_w_out_time: float32 [576, 1152], P('seq', 'dp')
All inputs are finite; a program needn't handle non-finite values.
Results may differ from a plain program's by a relative error of at most 0.025.
Values may be sent and summed in bfloat16 or wider, within the bound.
A program may use at most 64 MiB of HBM per device.

v0:
```python
import math

import jax
import jax.numpy as jnp
from jax import lax
from jax.sharding import PartitionSpec as P

HEADS = 8
HD = 72


def for_sending(shard):

    def short(part):
        return part.astype(jnp.bfloat16) if part.dtype == jnp.float32 else part

    return jax.tree.map(short, shard)


def normalize(values):
    wide = values.astype(jnp.float32)
    scale = lax.rsqrt(jnp.mean(wide * wide, axis=-1, keepdims=True) + 1e-06)
    return (wide * scale).astype(jnp.bfloat16)


def attend(inputs, w_qkv, w_out):
    outer, rows, inner, width = inputs.shape
    normed = normalize(inputs).reshape(-1, width)
    packed = jnp.dot(normed, w_qkv, preferred_element_type=jnp.float32).astype(jnp.bfloat16)
    packed = packed.reshape(outer, rows, inner, 3, HEADS, HD)
    query = packed[:, :, :, 0]
    keys = packed[:, :, :, 1]
    values = packed[:, :, :, 2]
    scores = jnp.einsum(
        "arbhk,asbhk->abhrs", query, keys, preferred_element_type=jnp.float32
    ) / math.sqrt(HD)
    peak = jnp.max(scores, axis=-1, keepdims=True)
    expo = jnp.exp(scores - peak)
    probs = (expo / jnp.sum(expo, axis=-1, keepdims=True)).astype(jnp.bfloat16)
    mixed = jnp.einsum(
        "abhrs,asbhk->arbhk", probs, values, preferred_element_type=jnp.float32
    ).astype(jnp.bfloat16)
    mixed = mixed.reshape(outer, rows, inner, HEADS * HD)
    result = jnp.dot(
        mixed.reshape(-1, HEADS * HD), w_out, preferred_element_type=jnp.float32
    ).astype(jnp.bfloat16)
    return (result.reshape(inputs.shape), mixed)


def body(
    y_first, y_second, grad_first, grad_second, w_qkv_space, w_out_space, w_qkv_time, w_out_time
):
    part_a, part_b, part_c, part_d = (
        lax.all_gather(w_qkv_space, "seq", axis=0, tiled=True),
        lax.all_gather(w_out_space, "seq", axis=0, tiled=True),
        lax.all_gather(w_qkv_time, "seq", axis=0, tiled=True),
        lax.all_gather(w_out_time, "seq", axis=0, tiled=True),
    )
    space_qkv, space_proj, time_qkv, time_proj = (
        lax.all_gather(part_a, "dp", axis=1, tiled=True),
        lax.all_gather(part_b, "dp", axis=1, tiled=True),
        lax.all_gather(part_c, "dp", axis=1, tiled=True),
        lax.all_gather(part_d, "dp", axis=1, tiled=True),
    )
    frame_count = y_first.shape[1]
    tokens = y_first.shape[2]
    width = y_first.shape[3]

    def time_fn(inputs):
        return attend(inputs, time_qkv, time_proj)

    def space_fn(inputs):
        return attend(inputs, space_qkv, space_proj)[0]

    first_patch = lax.all_to_all(y_first, "seq", split_axis=2, concat_axis=1, tiled=True)
    time_out, time_vjp, time_mixed = jax.vjp(time_fn, first_patch, has_aux=True)
    time_frames = jax.tree.map(
        lambda part, own: part.astype(own.dtype),
        lax.all_to_all(for_sending(time_out), "seq", split_axis=1, concat_axis=2, tiled=True),
        time_out,
    )
    second_in = (y_second.astype(jnp.float32) - time_frames.astype(jnp.float32)).astype(
        jnp.bfloat16
    )
    space_out, space_vjp = jax.vjp(space_fn, second_in.reshape(frame_count, tokens, 1, width))
    first_in = (
        y_first.astype(jnp.float32) - space_out.reshape(y_first.shape).astype(jnp.float32)
    ).astype(jnp.bfloat16)
    cot_patch = lax.all_to_all(grad_second, "seq", split_axis=2, concat_axis=1, tiled=True)
    back_patch = time_vjp(cot_patch)[0]
    back_frames = jax.tree.map(
        lambda part, own: part.astype(own.dtype),
        lax.all_to_all(for_sending(back_patch), "seq", split_axis=1, concat_axis=2, tiled=True),
        back_patch,
    )
    first_grad = (grad_first.astype(jnp.float32) + back_frames.astype(jnp.float32)).astype(
        jnp.bfloat16
    )
    back_space = space_vjp(first_grad.reshape(frame_count, tokens, 1, width))[0]
    second_grad = (
        grad_second.astype(jnp.float32) + back_space.reshape(y_first.shape).astype(jnp.float32)
    ).astype(jnp.bfloat16)
    partial_grad = lax.dot_general(
        time_mixed.reshape(-1, time_mixed.shape[3]),
        cot_patch.reshape(-1, width),
        (((0,), (0,)), ((), ())),
        preferred_element_type=jnp.float32,
    )
    row_share = lax.psum_scatter(partial_grad, "seq", scatter_dimension=0, tiled=True)
    grad_share = lax.psum_scatter(
        row_share.astype(jnp.bfloat16), "dp", scatter_dimension=1, tiled=True
    ).astype(jnp.float32)
    return (first_in, second_in, first_grad, second_grad, grad_share)


def solution(mesh):
    placed = (
        P("dp", "seq", None, None),
        P("dp", "seq", None, None),
        P("dp", "seq", None, None),
        P("dp", "seq", None, None),
        P("seq", "dp"),
        P("seq", "dp"),
        P("seq", "dp"),
        P("seq", "dp"),
    )
    return jax.shard_map(
        body,
        mesh=mesh,
        in_specs=placed,
        out_specs=(
            P("dp", "seq", None, None),
            P("dp", "seq", None, None),
            P("dp", "seq", None, None),
            P("dp", "seq", None, None),
            P("seq", "dp"),
        ),
        check_vma=False,
    )
```

profile of v0, /device:TPU:0, one launch (start us, length us, event | category | flops | bytes accessed | tf_op | source)
XLA Modules:
  0.0 370.5 jit_solution(6612292458136604578)
XLA Ops:
  7.2 0.7 all-gather.9.cloned.1.call-update
  8.0 66.0 %all-gather.9.cloned.1.call-done = bf16[1152,864]{1,0:T(8,128)(2,1)} async-done(((bf16[72,864]{1,0:T(8,128)(2,1)}), bf16[1152,864]{1,0:T(8,128)(2,1)}) %all-gather.9.cloned.1.call-update) | async-done | bytes 1990672 | tf_op jit(solution)/shard_map/all_gather | solution.py:56
  73.9 4.1 %copy.90 = bf16[1152,864]{0,1:T(8,128)(2,1)} copy(bf16[1152,864]{1,0:T(8,128)(2,1)} %all-gather.9.cloned.1.call-done) | data formatting | bytes 3981312 | tf_op jit(solution)/shard_map/all_gather | solution.py:56
  78.1 43.6 %all-gather = bf16[16,36,576]{2,1,0:T(8,128)(2,1)S(1)} all-gather(bf16[1,36,576]{2,1,0:T(8,128)(2,1)S(1)} %bitcast.192), channel_id=1, replica_groups=mesh['dp'=2,'seq'=16] {'seq'}, dimensions={0}, use_global_device_ids=true | all-gather | bytes 705024 | tf_op jit(solution)/shard_map/all_gather | solution.py:57
  122.0 1.2 copy.97
  123.3 1.0 copy.88
  124.3 3.5 all-to-all-start
  127.9 1.0 copy.108
  128.9 7.7 %all-to-all-done = bf16[1,2,64,1152]{3,1,0,2:T(2,128)(2,1)S(1)} async-done(((bf16[1,2,64,1152]{3,1,0,2:T(2,128)(2,1)}), bf16[1,2,64,1152]{3,1,0,2:T(2,128)(2,1)S(1)}, u32[]{:S(2)}, u32[]{:S(2)}) %all-to-all-start) | async-done | bytes 294944 | tf_op jit(solution)/shard_map/all_to_all | solution.py:75
  136.6 5.6 %all-to-all-start.2 = ((bf16[1,2,64,1152]{3,1,0,2:T(2,128)(2,1)}), bf16[1,2,64,1152]{3,1,0,2:T(2,128)(2,1)S(1)}, u32[]{:S(2)}, u32[]{:S(2)}) async-start(bf16[1,2,64,1152]{3,1,0,2:T(2,128)(2,1)} %copy.108), calls=%async_computation.2 | async-start | bytes 589824 | tf_op jit(solution)/shard_map/all_to_all | solution.py:89
  143.4 0.6 multiply_add_fusion
  144.3 6.6 %all-to-all-done.2 = bf16[1,2,64,1152]{3,1,0,2:T(2,128)(2,1)S(1)} async-done(((bf16[1,2,64,1152]{3,1,0,2:T(2,128)(2,1)}), bf16[1,2,64,1152]{3,1,0,2:T(2,128)(2,1)S(1)}, u32[]{:S(2)}, u32[]{:S(2)}) %all-to-all-start.2) | async-done | bytes 294944 | tf_op jit(solution)/shard_map/all_to_all | solution.py:89
  151.1 0.8 reshape.550
  151.8 3.4 convolution_convert_fusion.3
  155.5 0.9 reshape.539
  156.9 0.7 copy-done.2
  158.1 0.9 reshape.543
  158.9 1.6 fusion.62
  160.5 83.1 %fusion = f32[48,1152]{1,0:T(8,128)} fusion(f32[576,1152]{1,0:T(8,128)S(1)} %fusion.62), kind=kCustom, calls=%all-reduce-scatter | all-reduce-scatter fusion | flops 884737 | bytes 2875904
  243.6 0.9 convert.36
  244.6 1.3 collective-permute-start
  245.9 2.3 collective-permute-start.1
  248.2 5.9 %collective-permute-start.2 = (bf16[48,1152]{1,0:T(8,128)(2,1)S(1)}, bf16[48,1152]{1,0:T(8,128)(2,1)S(1)}, u32[]{:S(2)}, u32[]{:S(2)}) collective-permute-start(bf16[48,1152]{1,0:T(8,128)(2,1)S(1)} %convert.36), channel_id=1, source_target_pairs={{0,3},{1,4},{2,5},{3,6},{4,7},{5,8},{6,9},{7,10},{8,11},{9,12},{10... | collective-permute-start | bytes 331784
  254.1 0.9 slice.30
  255.1 1.8 collective-permute-start.3
  256.9 1.3 dynamic-slice.4
  259.4 1.9 concatenate
  261.3 0.9 copy.126
  262.3 43.2 %all-gather.1 = bf16[16,36,576]{2,1,0:T(8,128)(2,1)S(1)} all-gather(bf16[1,36,576]{2,1,0:T(8,128)(2,1)} %bitcast.193), channel_id=1, replica_groups=mesh['dp'=2,'seq'=16] {'seq'}, dimensions={0}, use_global_device_ids=true | all-gather | bytes 705024 | tf_op jit(solution)/shard_map/all_gather | solution.py:55
  305.8 1.2 copy.107
  307.3 0.9 copy.89
  308.2 2.1 convolution_convert_fusion.17
  310.9 4.3 %copy.100 = bf16[1152,864]{0,1:T(8,128)(2,1)} copy(bf16[1152,864]{1,0:T(8,128)(2,1)} %all-gather.15.cloned.1.call-done) | data formatting | bytes 3981312 | tf_op jit(solution)/shard_map/all_gather | solution.py:54
  318.0 2.9 fusion.2
  321.1 1.0 reshape.562
  322.4 2.4 fusion.13
  324.8 3.5 all-to-all-start.3
  328.9 0.8 reshape.544
  329.7 1.0 copy.127
  330.7 0.7 convert_element_type.459
  331.4 5.6 %all-to-all-done.3 = bf16[1,32,4,1152]{3,2,0,1:T(4,128)(2,1)S(1)} async-done(((bf16[1,32,4,1152]{3,2,0,1:T(4,128)(2,1)}), bf16[1,32,4,1152]{3,2,0,1:T(4,128)(2,1)S(1)}, u32[]{:S(2)}, u32[]{:S(2)}) %all-to-all-start.3) | async-done | bytes 294944 | tf_op jit(solution)/shard_map/all_to_all | solution.py:93
  337.0 3.8 %all-to-all-start.1 = ((bf16[1,32,4,1152]{3,2,0,1:T(4,128)(2,1)}), bf16[1,32,4,1152]{3,2,0,1:T(4,128)(2,1)S(1)}, u32[]{:S(2)}, u32[]{:S(2)}) async-start(bf16[1,32,4,1152]{3,2,0,1:T(4,128)(2,1)} %bitcast.8), calls=%async_computation.1 | async-start | bytes 589824 | tf_op jit(solution)/shard_map/all_to_all | solution.py:79
  341.2 2.1 convolution_convert_fusion.16
  343.8 5.5 %all-to-all-done.1 = bf16[1,32,4,1152]{3,2,0,1:T(4,128)(2,1)S(1)} async-done(((bf16[1,32,4,1152]{3,2,0,1:T(4,128)(2,1)}), bf16[1,32,4,1152]{3,2,0,1:T(4,128)(2,1)S(1)}, u32[]{:S(2)}, u32[]{:S(2)}) %all-to-all-start.1) | async-done | bytes 294944 | tf_op jit(solution)/shard_map/all_to_all | solution.py:79
  350.1 3.3 convolution_convert_fusion.2
  353.8 0.6 fusion.56
  358.4 3.0 fusion.1
  362.5 1.1 fusion.15
  (138 shorter events, 15.5 us)
Async XLA Ops:
  7.2 66.8 %all-gather.9.cloned.1.call-start = ((), (), s32[]{:S(2)}) async-start(), calls=%async_computation.5 | async-start | bytes 2193408 | tf_op jit(solution)/shard_map/all_gather | solution.py:56
  7.9 70.2 %copy-start.23 = (bf16[36,576]{1,0:T(8,128)(2,1)S(1)}, bf16[36,576]{1,0:T(8,128)(2,1)}, u32[]{:S(2)}) copy-start(bf16[36,576]{1,0:T(8,128)(2,1)} %param.15) | copy-start | bytes 124420
  7.9 143.9 %all-gather.11.cloned.1.call-start = ((), (), s32[]{:S(2)}) async-start(), calls=%async_computation.6 | async-start | bytes 5971968 | tf_op jit(solution)/shard_map/all_gather | solution.py:62
  78.0 45.3 %copy-start.11 = (bf16[1,2,64,1152]{3,2,1,0:T(8,128)(2,1)S(1)}, bf16[1,2,64,1152]{3,2,1,0:T(8,128)(2,1)}, u32[]{:S(2)}) copy-start(bf16[1,2,64,1152]{3,2,1,0:T(8,128)(2,1)} %param.8) | copy-start | bytes 884740
  78.0 230.2 %all-gather.13.cloned.1.call-start = ((), (), s32[]{:S(2)}) async-start(), calls=%async_computation.7 | async-start | bytes 2211840 | tf_op jit(solution)/shard_map/all_gather | solution.py:63
  121.7 6.1 %copy-start.13 = (bf16[1,2,64,1152]{3,2,1,0:T(8,128)(2,1)S(1)}, bf16[1,2,64,1152]{3,2,1,0:T(8,128)(2,1)}, u32[]{:S(2)}) copy-start(bf16[1,2,64,1152]{3,2,1,0:T(8,128)(2,1)} %param.11) | copy-start | bytes 884740
  124.3 12.3 %all-to-all-start = ((bf16[1,2,64,1152]{3,1,0,2:T(2,128)(2,1)}), bf16[1,2,64,1152]{3,1,0,2:T(2,128)(2,1)S(1)}, u32[]{:S(2)}, u32[]{:S(2)}) async-start(bf16[1,2,64,1152]{3,1,0,2:T(2,128)(2,1)} %copy.88), calls=%async_computation | async-start | bytes 589824 | tf_op jit(solution)/shard_map/all_to_all | solution.py:75
  136.6 14.3 %all-to-all-start.2 = ((bf16[1,2,64,1152]{3,1,0,2:T(2,128)(2,1)}), bf16[1,2,64,1152]{3,1,0,2:T(2,128)(2,1)S(1)}, u32[]{:S(2)}, u32[]{:S(2)}) async-start(bf16[1,2,64,1152]{3,1,0,2:T(2,128)(2,1)} %copy.108), calls=%async_computation.2 | async-start | bytes 589824 | tf_op jit(solution)/shard_map/all_to_all | solution.py:89
  142.2 168.6 %all-gather.15.cloned.1.call-start = ((), (), s32[]{:S(2)}) async-start(), calls=%async_computation.8 | async-start | bytes 2193408 | tf_op jit(solution)/shard_map/all_gather | solution.py:54
  142.8 186.9 %reduce-scatter.6.cloned.1.call-start = ((), (), s32[]{:S(2)}) async-start(), calls=%async_computation.11 | async-start | bytes 442368
  156.5 1.4 copy-start.6
  156.5 1.4 copy-start.8
  156.5 1.4 copy-start.18
  156.8 0.8 copy-start.2
  156.9 0.7 copy-start.20
  244.6 14.8 %collective-permute-start = (bf16[48,1152]{1,0:T(8,128)(2,1)S(1)}, bf16[48,1152]{1,0:T(8,128)(2,1)S(1)}, u32[]{:S(2)}, u32[]{:S(2)}) collective-permute-start(bf16[48,1152]{1,0:T(8,128)(2,1)S(1)} %convert.36), channel_id=1, source_target_pairs={{0,1},{1,2},{2,3},{3,4},{4,5},{5,6},{6,7},{7,8},{8,9},{9,10},{10,1... | collective-permute-start | bytes 331784
  245.9 13.5 %collective-permute-start.1 = (bf16[48,1152]{1,0:T(8,128)(2,1)S(1)}, bf16[48,1152]{1,0:T(8,128)(2,1)S(1)}, u32[]{:S(2)}, u32[]{:S(2)}) collective-permute-start(bf16[48,1152]{1,0:T(8,128)(2,1)S(1)} %convert.36), channel_id=1, source_target_pairs={{0,2},{1,3},{2,4},{3,5},{4,6},{5,7},{6,8},{7,9},{8,10},{9,11},{10,... | collective-permute-start | bytes 331784
  248.2 11.2 %collective-permute-start.2 = (bf16[48,1152]{1,0:T(8,128)(2,1)S(1)}, bf16[48,1152]{1,0:T(8,128)(2,1)S(1)}, u32[]{:S(2)}, u32[]{:S(2)}) collective-permute-start(bf16[48,1152]{1,0:T(8,128)(2,1)S(1)} %convert.36), channel_id=1, source_target_pairs={{0,3},{1,4},{2,5},{3,6},{4,7},{5,8},{6,9},{7,10},{8,11},{9,12},{10... | collective-permute-start | bytes 331784
  255.1 4.3 %collective-permute-start.3 = (bf16[36,1152]{1,0:T(8,128)(2,1)S(1)}, bf16[36,1152]{1,0:T(8,128)(2,1)S(1)}, u32[]{:S(2)}, u32[]{:S(2)}) collective-permute-start(bf16[36,1152]{1,0:T(8,128)(2,1)S(1)} %slice.30), channel_id=1, source_target_pairs={{0,4},{1,5},{2,6},{3,7},{4,8},{5,9},{6,10},{7,11},{8,12},{9,13},{1... | collective-permute-start | bytes 248840
  262.2 79.0 %all-gather.19.cloned.1.call-start = ((), (), s32[]{:S(2)}) async-start(), calls=%async_computation.10 | async-start | bytes 2211840 | tf_op jit(solution)/shard_map/all_gather | solution.py:61
  262.3 45.9 %copy-start.5 = (bf16[128,1152]{1,0:T(8,128)(2,1)S(1)}, bf16[128,1152]{1,0:T(8,128)(2,1)}, u32[]{:S(2)}) copy-start(bf16[128,1152]{1,0:T(8,128)(2,1)} %reshape.550) | copy-start | bytes 884740
  307.0 43.0 %all-gather.17.cloned.1.call-start = ((), (), s32[]{:S(2)}) async-start(), calls=%async_computation.9 | async-start | bytes 5971968 | tf_op jit(solution)/shard_map/all_gather | solution.py:60
  310.8 4.4 %copy-start.21 = (f32[4,8,32]{2,1,0:T(8,128)S(1)}, f32[4,8,32]{2,1,0:T(8,128)}, u32[]{:S(2)}) copy-start(f32[4,8,32]{2,1,0:T(8,128)} %copy-done.20) | copy-start | bytes 12292
  310.8 4.4 %copy-start.3 = (f32[4,8,32,32]{2,3,1,0:T(8,128)S(1)}, f32[4,8,32,32]{2,3,1,0:T(8,128)}, u32[]{:S(2)}) copy-start(f32[4,8,32,32]{2,3,1,0:T(8,128)} %copy-done.2) | copy-start | bytes 393220
  310.8 4.4 %copy-start.19 = (bf16[1,32,4,1,8,72]{5,4,3,2,1,0:T(8,128)(2,1)S(1)}, bf16[1,32,4,1,8,72]{5,4,3,2,1,0:T(8,128)(2,1)}, u32[]{:S(2)}) copy-start(bf16[1,32,4,1,8,72]{5,4,3,2,1,0:T(8,128)(2,1)} %copy-done.18) | copy-start | bytes 442372
  315.1 0.9 copy-start.9
  315.2 1.2 copy-start.7
  320.9 1.4 copy-start.22
  320.9 7.4 %copy-start = (bf16[576,1152]{0,1:T(8,128)(2,1)S(1)}, bf16[576,1152]{0,1:T(8,128)(2,1)}, u32[]{:S(2)}) copy-start(bf16[576,1152]{0,1:T(8,128)(2,1)} %all-gather.13.cloned.1.call-done) | copy-start | bytes 3981316
  320.9 7.4 %copy-start.10 = (bf16[128,576]{1,0:T(8,128)(2,1)S(1)}, bf16[128,576]{1,0:T(8,128)(2,1)}, u32[]{:S(2)}) copy-start(bf16[128,576]{1,0:T(8,128)(2,1)} %reshape.543) | copy-start | bytes 442372
  324.8 12.2 %all-to-all-start.3 = ((bf16[1,32,4,1152]{3,2,0,1:T(4,128)(2,1)}), bf16[1,32,4,1152]{3,2,0,1:T(4,128)(2,1)S(1)}, u32[]{:S(2)}, u32[]{:S(2)}) async-start(bf16[1,32,4,1152]{3,2,0,1:T(4,128)(2,1)} %fusion.13), calls=%async_computation.3 | async-start | bytes 589824 | tf_op jit(solution)/shard_map/all_to_all | solution.py:93
  328.9 12.2 %copy-start.16 = (bf16[1,2,64,1152]{3,2,1,0:T(8,128)(2,1)S(1)}, bf16[1,2,64,1152]{3,2,1,0:T(8,128)(2,1)}, u32[]{:S(2)}) copy-start(bf16[1,2,64,1152]{3,2,1,0:T(8,128)(2,1)} %param.10) | copy-start | bytes 884740
  337.0 12.3 %all-to-all-start.1 = ((bf16[1,32,4,1152]{3,2,0,1:T(4,128)(2,1)}), bf16[1,32,4,1152]{3,2,0,1:T(4,128)(2,1)S(1)}, u32[]{:S(2)}, u32[]{:S(2)}) async-start(bf16[1,32,4,1152]{3,2,0,1:T(4,128)(2,1)} %bitcast.8), calls=%async_computation.1 | async-start | bytes 589824 | tf_op jit(solution)/shard_map/all_to_all | solution.py:79
  341.2 8.5 %copy-start.15 = (bf16[1,2,64,1152]{3,2,1,0:T(8,128)(2,1)}, bf16[1,2,64,1152]{3,2,1,0:T(8,128)(2,1)S(1)}, u32[]{:S(2)}) copy-start(bf16[1,2,64,1152]{3,2,1,0:T(8,128)(2,1)S(1)} %add_convert_fusion.1) | copy-start | bytes 884740
  341.2 8.4 %copy-start.17 = (bf16[1,2,64,1152]{3,2,1,0:T(8,128)(2,1)S(1)}, bf16[1,2,64,1152]{3,2,1,0:T(8,128)(2,1)}, u32[]{:S(2)}) copy-start(bf16[1,2,64,1152]{3,2,1,0:T(8,128)(2,1)} %param.9) | copy-start | bytes 884740
  349.8 12.7 %copy-start.4 = (bf16[1,2,64,1152]{3,2,1,0:T(8,128)(2,1)}, bf16[1,2,64,1152]{3,2,1,0:T(8,128)(2,1)S(1)}, u32[]{:S(2)}) copy-start(bf16[1,2,64,1152]{3,2,1,0:T(8,128)(2,1)S(1)} %get-tuple-element.14) | copy-start | bytes 884740
  358.3 3.6 copy-start.1
  361.4 1.1 copy-start.12
  361.4 1.1 copy-start.14
Sparse Core Ops, SparseCore 0:
  10.7 63.1 all-gather.8
  78.2 12.0 all-gather.10
  123.4 5.5 all-gather.12
  145.4 78.5 all-gather.14
  262.4 6.9 reduce-scatter.5
  307.2 5.5 all-gather.18
  315.3 13.5 all-gather.16
where the time goes:
time: 372 us; the launch traced here: 370 us
  blocking collectives  170 us (46%)
  waiting for transfers between devices  93.4 us (25%)
  local copies, waits for them, and re-layouts  32.2 us (9%)
  starting transfers between devices  28.3 us (8%)
  matrix products  23.1 us (6%)
  between operations  15.6 us (4%)
  other arithmetic  8.08 us (2%)
    unnamed x1, blocking collectives  83.1 us
    all_gather x1, waiting for transfers between devices, body(): lax.all_gather(w_qkv_time, 'seq', axis=0, tiled=True)  66 us
    all_gather x1, blocking collectives, body(): lax.all_gather(w_out_time, 'seq', axis=0, tiled=True)  43.6 us
    all_gather x1, blocking collectives, body(): lax.all_gather(w_out_space, 'seq', axis=0, tiled=True)  43.2 us
    unnamed x62, local copies, waits for them, and re-layouts  12.7 us
    dot_general x4, matrix products, attend(): jnp.dot(normed, w_qkv, preferred_element_type=jnp.float32)  12.6 us
    unnamed x5, starting transfers between devices  11.4 us
    all_to_all x1, waiting for transfers between devices, body(): lax.all_to_all(y_first, 'seq', split_axis=2, concat_axis=1, tiled=True)  7.73 us
  transfers between devices with their start and end apart: 15, of which 6 were waited for; matrix products, arithmetic and copies ran while one was open for 35% of the time, Pallas kernels for 0%

commit v1 on v0

v1 whole, which is shorter than its diff:
```python
import functools
import math

import jax
import jax.numpy as jnp
from jax import lax
from jax.experimental import pallas as pl
from jax.experimental.pallas import tpu as pltpu
from jax.sharding import PartitionSpec as P

HEADS = 8
HD = 72
WIDE = HEADS * HD
F32 = jnp.float32
BF16 = jnp.bfloat16
MESH = pl.DeviceIdType.MESH


def mm(a, b):
    return lax.dot_general(a, b, (((1,), (0,)), ((), ())), preferred_element_type=F32)


def mm_nt(a, b):
    return lax.dot_general(a, b, (((1,), (1,)), ((), ())), preferred_element_type=F32)


def mm_tn(a, b):
    return lax.dot_general(a, b, (((0,), (0,)), ((), ())), preferred_element_type=F32)


def whole(count):
    return (count + 15) // 16 * 16


def one_hot(rows, columns, target):
    place = target(lax.broadcasted_iota(jnp.int32, (rows, 1), 0))
    column = lax.broadcasted_iota(jnp.int32, (rows, columns), 1)
    return jnp.where(column == place, 1.0, 0.0).astype(BF16)


def columns_of(parts, count):
    joined = jnp.concatenate(parts, axis=1) if len(parts) > 1 else parts[0]
    each = joined.shape[1] // count
    return [joined[:, i * each : (i + 1) * each] for i in range(count)]


def forward(x, w_in, w_out, spread_in, spread_out, same):
    tokens = x.shape[0]
    scale = lax.rsqrt(jnp.mean(x * x, axis=-1, keepdims=True) + 1e-06)
    normed = mm((x * scale).astype(BF16), spread_in).astype(BF16)
    query, keys, values = columns_of([mm(normed, w()) for w in w_in], 3)
    query = by_head(query, tokens).astype(BF16)
    scores = mm_nt(query, keys.astype(BF16)) * (1.0 / math.sqrt(HD))
    scores = scores.reshape(HEADS, tokens, tokens)
    scores = jnp.where(same[None], scores, -1e30)
    expo = jnp.exp(scores - jnp.max(scores, axis=-1, keepdims=True))
    exact = expo / jnp.sum(expo, axis=-1, keepdims=True)
    probs = exact.reshape(HEADS * tokens, tokens).astype(BF16)
    mixed = mm(side_by_side(probs, tokens), by_head(values, tokens).astype(BF16)).astype(BF16)
    mixed = mm(mixed, spread_out).astype(BF16)
    result = columns_of([mm(mixed, w()) for w in w_out], 1)[0].astype(BF16)
    return result, mixed, (x, scale, query, keys, values.astype(BF16), probs)


def backward(saved, cotangent, w_in, w_out, spread_in, spread_out):
    x, scale, query, keys, values, probs = saved
    tokens = x.shape[0]
    pieces = columns_of([cotangent], len(w_out))
    d_mixed = sum(mm_nt(piece.astype(BF16), w()) for piece, w in zip(pieces, w_out))
    d_mixed = by_head(mm_nt(d_mixed.astype(BF16), spread_out), tokens).astype(BF16)
    d_values = mm_tn(probs, d_mixed)
    d_probs = mm_nt(d_mixed, values)
    weight = probs.astype(F32)
    inner = jnp.sum(d_probs * weight, axis=-1, keepdims=True)
    d_scores = (weight * (d_probs - inner) * (1.0 / math.sqrt(HD))).astype(BF16)
    d_query = mm(side_by_side(d_scores, tokens), by_head(keys, tokens).astype(BF16))
    d_keys = mm_tn(d_scores, query)
    pieces = columns_of([d_query, d_keys, d_values], len(w_in))
    d_normed = sum(mm_nt(piece.astype(BF16), w()) for piece, w in zip(pieces, w_in))
    d_normed = mm_nt(d_normed.astype(BF16), spread_in)
    inner = jnp.mean(d_normed * x, axis=-1, keepdims=True)
    return d_normed * scale - x * (scale * scale * scale * inner)


def block_kernel(
    n, ndp, frames, spots, rows_in, rows_out,
    y1_ref, y2_ref, g1_ref, g2_ref, ws_ref, os_ref, wt_ref, ot_ref,
    x1_ref, x2_ref, d1_ref, d2_ref, gw_ref,
    w_buf, o_buf, sent, arrived, answer, returned, g_part, g_chip, g_sent, g_arrived,
    w_recv, w_share, p_recv, g_share, send_sems,
):
    quad = 4 if n % 4 == 0 else 1
    line = n // quad
    me_d, me = lax.axis_index("dp"), lax.axis_index("seq")
    z, q = me // quad, me % quad
    x_side, y_side = q + 1 - 2 * (q % 2), (q + 2) % quad
    far = (x_side + 2) % quad
    tokens, width = y1_ref.shape
    per = spots // n
    half = frames * per
    slot = sent.shape[1]
    others = [lax.rem(me + k, n) for k in range(1, n)]
    mates = [lax.rem(me_d + k, ndp) for k in range(1, ndp)]
    first_in, first_out = whole(rows_in), whole(rows_out)
    spans = [
        [(0, first_in), (0, first_out)],
        [(first_in, w_buf.shape[3]), (first_out, o_buf.shape[3])],
    ]
    pending = []

    barrier = pltpu.get_barrier_semaphore()
    for s in others:
        pl.semaphore_signal(barrier, inc=1, device_id=(me_d, s), device_id_type=MESH)
    for d in mates:
        pl.semaphore_signal(barrier, inc=1, device_id=(d, me), device_id_type=MESH)

    def copy(source, target, sem, device):
        made = pltpu.make_async_remote_copy(
            src_ref=source, dst_ref=target, send_sem=send_sems.at[len(pending)],
            recv_sem=sem, device_id=device, device_id_type=MESH,
        )
        made.start()
        pending.append(made)

    def await_into(target, sem):
        pltpu.make_async_remote_copy(
            src_ref=target, dst_ref=target, send_sem=send_sems.at[0], recv_sem=sem,
            device_id=(me_d, others[0]), device_id_type=MESH,
        ).wait_recv()

    def part(phase, kind, zz, qq):
        low, high = spans[phase][kind]
        return (w_buf, o_buf)[kind].at[me_d, zz, qq, low:high, :]

    def line_of(phase, kind, d, qq):
        low, high = spans[phase][kind]
        return (w_buf, o_buf)[kind].at[d, :, qq, low:high, :]

    def pass_on(phase, zz, qq, to_z, to_q):
        for kind in range(2):
            block = part(phase, kind, zz, qq)
            sem = w_recv.at[2 * phase + kind, zz, qq]
            copy(block, block, sem, (me_d, to_z * quad + to_q))

    def landed(phase, zz, qq):
        for kind in range(2):
            await_into(part(phase, kind, zz, qq), w_recv.at[2 * phase + kind, zz, qq])

    def to_mates(phase, qq):
        for kind in range(2):
            block = line_of(phase, kind, me_d, qq)
            for d in mates:
                copy(block, block, w_share.at[2 * phase + kind, me_d, qq], (d, me))

    def spread_own(phase):
        for k in range(1, line):
            pass_on(phase, z, q, lax.rem(z + k, line), q)
        pass_on(phase, z, q, z, x_side)
        pass_on(phase, z, q, z, y_side)

    def spread_line(phase):
        for k in range(1, line):
            zz = lax.rem(z + line - k, line)
            landed(phase, zz, q)
            pass_on(phase, zz, q, z, x_side)
            pass_on(phase, zz, q, z, y_side)
        to_mates(phase, q)

    def spread_far(phase):
        for k in range(line):
            zz = lax.rem(z + line - k, line)
            landed(phase, zz, x_side)
            landed(phase, zz, y_side)
            if k % 2 == 0:
                pass_on(phase, zz, x_side, z, y_side)
            else:
                pass_on(phase, zz, y_side, z, x_side)
        to_mates(phase, x_side)
        to_mates(phase, y_side)

    def finish(phase):
        for zz in range(line):
            landed(phase, zz, far)
        to_mates(phase, far)
        for d in mates:
            for qq in range(quad):
                for kind in range(2):
                    await_into(
                        line_of(phase, kind, d, qq), w_share.at[2 * phase + kind, d, qq]
                    )

    for buf, time_ref, space_ref in ((w_buf, wt_ref, ws_ref), (o_buf, ot_ref, os_ref)):
        count, depth = time_ref.shape[0], buf.shape[3]
        place_time = one_hot(count, depth, lambda r: r)
        place_space = one_hot(count, depth, lambda r: r + count)
        block = mm_tn(place_time, time_ref[...]) + mm_tn(place_space, space_ref[...])
        buf[me_d, z, q] = block.astype(BF16)

    def piece(o):
        return one_hot(
            tokens,
            n * slot,
            lambda t: (t % spots // per) * slot + (o * frames + t // spots) * per + t % per,
        )

    def arrival(o):
        return one_hot(tokens, n * slot, lambda r: (r // half) * slot + o * half + r % half)

    spots_first, spots_second = piece(0), piece(1)
    packed = mm_tn(spots_first, y1_ref[...]) + mm_tn(spots_second, g2_ref[...])
    sent[...] = packed.astype(BF16).reshape(sent.shape)

    pl.semaphore_wait(barrier, n - 1 + ndp - 1)

    def exchange(source, target, row):
        for s in others:
            copy(source.at[s], target.at[me], p_recv.at[row, me], (me_d, s))
        target[me] = source[me]

    def exchanged(target, row):
        for s in others:
            await_into(target.at[s], p_recv.at[row, s])

    spread_own(0)
    exchange(sent, arrived, 0)
    spread_line(0)
    spread_far(0)
    finish(0)
    spread_own(1)
    exchanged(arrived, 0)

    def groups(mark):
        row = mark(lax.broadcasted_iota(jnp.int32, (tokens, 1), 0))
        column = mark(lax.broadcasted_iota(jnp.int32, (1, tokens), 1))
        return row == column

    def weights(buf, low, high):
        def one(d):
            return lambda: buf[d, :, :, low:high, :].reshape(n * (high - low), buf.shape[4])

        return [one(d) for d in range(ndp)]

    def spreads(low_in, depth_in, low_out, depth_out):
        return (
            one_hot(width, n * depth_in, lambda c: c // rows_in * depth_in + low_in + c % rows_in),
            one_hot(WIDE, n * depth_out, lambda c: c // rows_out * depth_out + low_out + c % rows_out),
        )

    rows = arrived[...].reshape(n * slot, width)
    take_first, take_second = arrival(0), arrival(1)
    cotangent = mm(take_second, rows)
    w_in, w_out = weights(w_buf, 0, first_in), weights(o_buf, 0, first_out)
    spread_in, spread_out = spreads(0, first_in, 0, first_out)
    result, mixed, saved = forward(
        mm(take_first, rows), w_in, w_out, spread_in, spread_out, groups(lambda r: r % per)
    )
    spread_line(1)
    back = backward(saved, cotangent, w_in, w_out, spread_in, spread_out).astype(BF16)
    packed = mm_tn(take_first, result) + mm_tn(take_second, back)
    answer[...] = packed.astype(BF16).reshape(answer.shape)
    exchange(answer, returned, 1)
    for d, piece_of in enumerate(columns_of([cotangent], ndp)):
        g_part[d] = mm_tn(mixed, piece_of.astype(BF16)).astype(BF16)
    for d in mates:
        copy(g_part.at[d], g_chip.at[me_d], g_share.at[me_d], (d, me))
    g_chip[me_d] = g_part[me_d]
    spread_far(1)
    for d in mates:
        await_into(g_chip.at[d], g_share.at[d])
    total = g_chip[0].astype(F32)
    for d in range(1, ndp):
        total = total + g_chip[d].astype(F32)
    g_sent[...] = total.astype(BF16).reshape(g_sent.shape)
    exchange(g_sent, g_arrived, 2)

    exchanged(returned, 1)
    rows = returned[...].reshape(n * slot, width)
    x_second = (y2_ref[...].astype(F32) - mm(spots_first, rows)).astype(BF16)
    x2_ref[...] = x_second
    d_first = (g1_ref[...].astype(F32) + mm(spots_second, rows)).astype(BF16)
    d1_ref[...] = d_first
    finish(1)
    low_in, low_out = rows_in // 16 * 16, rows_out // 16 * 16
    high_in, high_out = whole(2 * rows_in), whole(2 * rows_out)
    w_in, w_out = weights(w_buf, low_in, high_in), weights(o_buf, low_out, high_out)
    spread_in, spread_out = spreads(
        rows_in - low_in, high_in - low_in, rows_out - low_out, high_out - low_out
    )
    result, _, saved = forward(
        x_second.astype(F32), w_in, w_out, spread_in, spread_out, groups(lambda t: t // spots)
    )
    x1_ref[...] = (y1_ref[...].astype(F32) - result.astype(F32)).astype(BF16)
    back = backward(saved, d_first.astype(F32), w_in, w_out, spread_in, spread_out)
    d2_ref[...] = (g2_ref[...].astype(F32) + back.astype(BF16).astype(F32)).astype(BF16)
    exchanged(g_arrived, 2)
    gw_ref[...] = jnp.sum(g_arrived[...].astype(F32), axis=0)[:rows_out]
    for made in pending:
        made.wait_send()


def body(n, ndp, *operands):
    shape = operands[0].shape
    frames, spots, width = shape[1:]
    tokens = frames * spots
    rows_in, columns_in = operands[4].shape
    rows_out, columns_out = operands[5].shape
    quad = 4 if n % 4 == 0 else 1
    line = n // quad
    slot = whole(2 * frames * spots // n)
    first_out = whole(rows_out)
    grad_rows = n * first_out
    per_phase = line - 1 + 2 + 2 * (line - 1) + line + quad * (ndp - 1)
    sends = 4 * per_phase + 3 * (n - 1) + ndp - 1
    like = jax.ShapeDtypeStruct((tokens, width), BF16)
    spec = pl.BlockSpec(memory_space=pltpu.VMEM)
    dma = pltpu.SemaphoreType.DMA
    outs = pl.pallas_call(
        functools.partial(block_kernel, n, ndp, frames, spots, rows_in, rows_out),
        out_shape=(like,) * 4 + (jax.ShapeDtypeStruct((rows_out, columns_out), F32),),
        in_specs=[spec] * 8,
        out_specs=[spec] * 5,
        scratch_shapes=[
            pltpu.VMEM((ndp, line, quad, whole(2 * rows_in), columns_in), BF16),
            pltpu.VMEM((ndp, line, quad, whole(2 * rows_out), columns_out), BF16),
            pltpu.VMEM((n, slot, width), BF16),
            pltpu.VMEM((n, slot, width), BF16),
            pltpu.VMEM((n, slot, width), BF16),
            pltpu.VMEM((n, slot, width), BF16),
            pltpu.VMEM((ndp, grad_rows, columns_out), BF16),
            pltpu.VMEM((ndp, grad_rows, columns_out), BF16),
            pltpu.VMEM((n, first_out, columns_out), BF16),
            pltpu.VMEM((n, first_out, columns_out), BF16),
            dma((4, line, quad)),
            dma((4, ndp, quad)),
            dma((3, n)),
            dma((ndp,)),
            dma((sends,)),
        ],
        compiler_params=pltpu.CompilerParams(
            collective_id=0, has_side_effects=True, vmem_limit_bytes=60 * 2**20
        ),
    )(*[part.reshape(tokens, width) for part in operands[:4]], *operands[4:])
    return tuple(part.reshape(shape) for part in outs[:4]) + (outs[4],)


def by_head(values, tokens):
    column = lax.broadcasted_iota(jnp.int32, (tokens, WIDE), 1)
    zero = jnp.zeros_like(values)
    return jnp.concatenate(
        [
            jnp.where((column >= h * HD) & (column < (h + 1) * HD), values, zero)
            for h in range(HEADS)
        ],
        axis=0,
    )


def side_by_side(stacked, tokens):
    return jnp.concatenate(
        [stacked[h * tokens : (h + 1) * tokens] for h in range(HEADS)], axis=1
    )


def solution(mesh):
    tokens = P("dp", "seq", None, None)
    weights = P("seq", "dp")
    return jax.shard_map(
        functools.partial(body, mesh.shape["seq"], mesh.shape["dp"]),
        mesh=mesh,
        in_specs=(tokens,) * 4 + (weights,) * 4,
        out_specs=(tokens,) * 4 + (weights,),
        check_vma=False,
    )
```

time: 372 us -> 116 us (0.31)
  the two profiles are of different devices: /device:TPU:0 before, /device:TPU:15 now
where the time goes in v1:
time: 116 us; the launch traced here: 115 us
  Pallas kernels  109 us (94%)
  local copies, waits for them, and re-layouts  5.49 us (5%)
    pallas_call x1, Pallas kernels, body(): pl.pallas_call(functools.partial(block_kernel, n, ndp, frames, spots, row...  109 us
    unnamed x13, local copies, waits for them, and re-layouts  5.49 us

profile of v1, /device:TPU:15, one launch (start us, length us, event | category | flops | bytes accessed | tf_op | source)
XLA Modules:
  0.0 115.3 jit_solution(11430569153306144967)
XLA Ops:
  0.6 109.1 %shard_map.119 = (bf16[128,1152]{1,0:T(8,128)(2,1)}, bf16[128,1152]{1,0:T(8,128)(2,1)}, bf16[128,1152]{1,0:T(8,128)(2,1)}, bf16[128,1152]{1,0:T(8,128)(2,1)}, f32[36,576]{1,0:T(8,128)}) custom-call(bf16[128,1152]{1,0:T(8,128)(2,1)} %bitcast.12, bf16[128,1152]{1,0:T(8,128)(2,1)} %bitcast.13, bf16[128,1152]{1,0:T(8,128)(2,1)} %bitcast.14, ...), custom_call_target="tpu_custom_call" | custom-call | tf_op jit(solution)/shard_map/pallas_call | solution.py:317
  109.8 0.0 copy-start.2
  109.8 1.7 %copy.18 = bf16[1,2,64,1152]{3,2,1,0:T(8,128)(2,1)} copy(bf16[1,2,64,1152]{3,2,1,0:T(8,128)(2,1)} %bitcast.11) | data formatting | bytes 589824
  111.5 0.0 copy-done.2
  111.5 0.0 copy-start.1
  111.5 0.7 copy.19
  112.2 0.4 copy-done.1
  112.6 0.0 copy-start
  112.6 0.7 copy.20
  113.3 0.4 copy-done
  113.7 0.0 copy-start.3
  113.7 0.7 copy.21
  114.4 0.2 copy-done.3
  114.6 0.6 copy.22
Async XLA Ops:
  109.8 1.8 %copy-start.2 = (bf16[128,1152]{1,0:T(8,128)(2,1)S(1)}, bf16[128,1152]{1,0:T(8,128)(2,1)}, u32[]{:S(2)}) copy-start(bf16[128,1152]{1,0:T(8,128)(2,1)} %get-tuple-element.11) | copy-start | bytes 884740
  111.5 1.1 copy-start.1
  112.6 1.1 copy-start
  113.7 1.0 copy-start.3

commit v2 on v1

--- a/solution.py
+++ b/solution.py
@@ -44,21 +44,24 @@
     return [joined[:, i * each : (i + 1) * each] for i in range(count)]
 
 
-def forward(x, w_in, w_out, spread_in, spread_out, same):
+def forward(x, w_in, w_out, spread_in, spread_out, same, ready_in, between, ready_out):
     tokens = x.shape[0]
     scale = lax.rsqrt(jnp.mean(x * x, axis=-1, keepdims=True) + 1e-06)
     normed = mm((x * scale).astype(BF16), spread_in).astype(BF16)
+    ready_in()
     query, keys, values = columns_of([mm(normed, w()) for w in w_in], 3)
     query = by_head(query, tokens).astype(BF16)
     scores = mm_nt(query, keys.astype(BF16)) * (1.0 / math.sqrt(HD))
+    between()
     scores = scores.reshape(HEADS, tokens, tokens)
     scores = jnp.where(same[None], scores, -1e30)
     expo = jnp.exp(scores - jnp.max(scores, axis=-1, keepdims=True))
     exact = expo / jnp.sum(expo, axis=-1, keepdims=True)
     probs = exact.reshape(HEADS * tokens, tokens).astype(BF16)
     mixed = mm(side_by_side(probs, tokens), by_head(values, tokens).astype(BF16)).astype(BF16)
-    mixed = mm(mixed, spread_out).astype(BF16)
-    result = columns_of([mm(mixed, w()) for w in w_out], 1)[0].astype(BF16)
+    spaced = mm(mixed, spread_out).astype(BF16)
+    ready_out()
+    result = columns_of([mm(spaced, w()) for w in w_out], 1)[0].astype(BF16)
     return result, mixed, (x, scale, query, keys, values.astype(BF16), probs)
 
 
@@ -84,10 +87,9 @@
 
 def block_kernel(
     n, ndp, frames, spots, rows_in, rows_out,
-    y1_ref, y2_ref, g1_ref, g2_ref, ws_ref, os_ref, wt_ref, ot_ref,
-    x1_ref, x2_ref, d1_ref, d2_ref, gw_ref,
-    w_buf, o_buf, sent, arrived, answer, returned, g_part, g_chip, g_sent, g_arrived,
-    w_recv, w_share, p_recv, g_share, send_sems,
+    y1_ref, y2_ref, g1_ref, g2_ref, ws_ref, os_ref, wt_ref, ot_ref, out_ref, gw_ref,
+    w_buf, o_buf, sent, arrived, answer, returned, g_part, g_chip, g_sent, g_quad, g_mid, g_line,
+    w_recv, w_share, p_recv, g_share, g_recv, send_sems,
 ):
     quad = 4 if n % 4 == 0 else 1
     line = n // quad
@@ -102,9 +104,11 @@
     others = [lax.rem(me + k, n) for k in range(1, n)]
     mates = [lax.rem(me_d + k, ndp) for k in range(1, ndp)]
     first_in, first_out = whole(rows_in), whole(rows_out)
-    spans = [
-        [(0, first_in), (0, first_out)],
-        [(first_in, w_buf.shape[3]), (first_out, o_buf.shape[3])],
+    phases = [
+        (w_buf, 0, first_in),
+        (o_buf, 0, first_out),
+        (w_buf, first_in, w_buf.shape[3]),
+        (o_buf, first_out, o_buf.shape[3]),
     ]
     pending = []
 
@@ -128,33 +132,31 @@
             device_id=(me_d, others[0]), device_id_type=MESH,
         ).wait_recv()
 
-    def part(phase, kind, zz, qq):
-        low, high = spans[phase][kind]
-        return (w_buf, o_buf)[kind].at[me_d, zz, qq, low:high, :]
-
-    def line_of(phase, kind, d, qq):
-        low, high = spans[phase][kind]
-        return (w_buf, o_buf)[kind].at[d, :, qq, low:high, :]
+    def part(phase, zz, qq):
+        buf, low, high = phases[phase]
+        return buf.at[me_d, zz, qq, low:high, :]
+
+    def line_of(phase, d, qq):
+        buf, low, high = phases[phase]
+        return buf.at[d, :, qq, low:high, :]
 
     def pass_on(phase, zz, qq, to_z, to_q):
-        for kind in range(2):
-            block = part(phase, kind, zz, qq)
-            sem = w_recv.at[2 * phase + kind, zz, qq]
-            copy(block, block, sem, (me_d, to_z * quad + to_q))
+        block = part(phase, zz, qq)
+        copy(block, block, w_recv.at[phase, zz, qq], (me_d, to_z * quad + to_q))
 
     def landed(phase, zz, qq):
-        for kind in range(2):
-            await_into(part(phase, kind, zz, qq), w_recv.at[2 * phase + kind, zz, qq])
+        await_into(part(phase, zz, qq), w_recv.at[phase, zz, qq])
 
     def to_mates(phase, qq):
-        for kind in range(2):
-            block = line_of(phase, kind, me_d, qq)
-            for d in mates:
-                copy(block, block, w_share.at[2 * phase + kind, me_d, qq], (d, me))
-
-    def spread_own(phase):
+        block = line_of(phase, me_d, qq)
+        for d in mates:
+            copy(block, block, w_share.at[phase, me_d, qq], (d, me))
+
+    def own_line(phase):
         for k in range(1, line):
             pass_on(phase, z, q, lax.rem(z + k, line), q)
+
+    def own_sides(phase):
         pass_on(phase, z, q, z, x_side)
         pass_on(phase, z, q, z, y_side)
 
@@ -184,10 +186,7 @@
         to_mates(phase, far)
         for d in mates:
             for qq in range(quad):
-                for kind in range(2):
-                    await_into(
-                        line_of(phase, kind, d, qq), w_share.at[2 * phase + kind, d, qq]
-                    )
+                await_into(line_of(phase, d, qq), w_share.at[phase, d, qq])
 
     for buf, time_ref, space_ref in ((w_buf, wt_ref, ws_ref), (o_buf, ot_ref, os_ref)):
         count, depth = time_ref.shape[0], buf.shape[3]
@@ -206,12 +205,6 @@
     def arrival(o):
         return one_hot(tokens, n * slot, lambda r: (r // half) * slot + o * half + r % half)
 
-    spots_first, spots_second = piece(0), piece(1)
-    packed = mm_tn(spots_first, y1_ref[...]) + mm_tn(spots_second, g2_ref[...])
-    sent[...] = packed.astype(BF16).reshape(sent.shape)
-
-    pl.semaphore_wait(barrier, n - 1 + ndp - 1)
-
     def exchange(source, target, row):
         for s in others:
             copy(source.at[s], target.at[me], p_recv.at[row, me], (me_d, s))
@@ -220,14 +213,6 @@
     def exchanged(target, row):
         for s in others:
             await_into(target.at[s], p_recv.at[row, s])
-
-    spread_own(0)
-    exchange(sent, arrived, 0)
-    spread_line(0)
-    spread_far(0)
-    finish(0)
-    spread_own(1)
-    exchanged(arrived, 0)
 
     def groups(mark):
         row = mark(lax.broadcasted_iota(jnp.int32, (tokens, 1), 0))
@@ -246,54 +231,107 @@
             one_hot(WIDE, n * depth_out, lambda c: c // rows_out * depth_out + low_out + c % rows_out),
         )
 
+    pl.semaphore_wait(barrier, n - 1 + ndp - 1)
+    own_line(0)
+    own_sides(0)
+    spots_first, spots_second = piece(0), piece(1)
+    packed = mm_tn(spots_first, y1_ref[...]) + mm_tn(spots_second, g2_ref[...])
+    sent[...] = packed.astype(BF16).reshape(sent.shape)
+    exchange(sent, arrived, 0)
+    own_line(1)
+    spread_in, spread_out = spreads(0, first_in, 0, first_out)
+    spread_line(0)
+    own_line(2)
+    own_line(3)
+    spread_far(0)
+    own_sides(1)
+    spread_line(1)
+
+    exchanged(arrived, 0)
     rows = arrived[...].reshape(n * slot, width)
     take_first, take_second = arrival(0), arrival(1)
     cotangent = mm(take_second, rows)
+
+    def next_phases():
+        spread_far(1)
+        own_sides(2)
+        spread_line(2)
+        own_sides(3)
+        spread_line(3)
+
     w_in, w_out = weights(w_buf, 0, first_in), weights(o_buf, 0, first_out)
-    spread_in, spread_out = spreads(0, first_in, 0, first_out)
     result, mixed, saved = forward(
-        mm(take_first, rows), w_in, w_out, spread_in, spread_out, groups(lambda r: r % per)
-    )
-    spread_line(1)
+        mm(take_first, rows), w_in, w_out, spread_in, spread_out, groups(lambda r: r % per),
+        lambda: finish(0), next_phases, lambda: finish(1),
+    )
     back = backward(saved, cotangent, w_in, w_out, spread_in, spread_out).astype(BF16)
     packed = mm_tn(take_first, result) + mm_tn(take_second, back)
     answer[...] = packed.astype(BF16).reshape(answer.shape)
     exchange(answer, returned, 1)
+
+    depth = g_sent.shape[1]
+    by_quad = one_hot(
+        WIDE,
+        quad * depth,
+        lambda c: c // rows_out % quad * depth + c // (rows_out * quad) * rows_out + c % rows_out,
+    )
+    mixed = mm(mixed, by_quad).astype(BF16)
     for d, piece_of in enumerate(columns_of([cotangent], ndp)):
-        g_part[d] = mm_tn(mixed, piece_of.astype(BF16)).astype(BF16)
+        g_part[d] = mm_tn(mixed, piece_of.astype(BF16)).astype(BF16).reshape(g_part.shape[1:])
     for d in mates:
         copy(g_part.at[d], g_chip.at[me_d], g_share.at[me_d], (d, me))
     g_chip[me_d] = g_part[me_d]
-    spread_far(1)
+    spread_far(2)
     for d in mates:
         await_into(g_chip.at[d], g_share.at[d])
     total = g_chip[0].astype(F32)
     for d in range(1, ndp):
         total = total + g_chip[d].astype(F32)
-    g_sent[...] = total.astype(BF16).reshape(g_sent.shape)
-    exchange(g_sent, g_arrived, 2)
+    g_sent[...] = total.astype(BF16)
+    for k in range(1, quad):
+        qq = lax.rem(q + k, quad)
+        copy(g_sent.at[qq], g_quad.at[q], g_recv.at[q], (me_d, z * quad + qq))
+    g_quad[q] = g_sent[q]
+    low_in, low_out = rows_in // 16 * 16, rows_out // 16 * 16
+    high_in, high_out = whole(2 * rows_in), whole(2 * rows_out)
+    spread_in, spread_out = spreads(
+        rows_in - low_in, high_in - low_in, rows_out - low_out, high_out - low_out
+    )
+    spread_far(3)
 
     exchanged(returned, 1)
     rows = returned[...].reshape(n * slot, width)
     x_second = (y2_ref[...].astype(F32) - mm(spots_first, rows)).astype(BF16)
-    x2_ref[...] = x_second
+    out_ref[1] = x_second
     d_first = (g1_ref[...].astype(F32) + mm(spots_second, rows)).astype(BF16)
-    d1_ref[...] = d_first
-    finish(1)
-    low_in, low_out = rows_in // 16 * 16, rows_out // 16 * 16
-    high_in, high_out = whole(2 * rows_in), whole(2 * rows_out)
+    out_ref[2] = d_first
+
+    def sum_quad():
+        for k in range(1, quad):
+            qq = lax.rem(q + k, quad)
+            await_into(g_quad.at[qq], g_recv.at[qq])
+        total = jnp.sum(g_quad[...].astype(F32), axis=0).astype(BF16)
+        regroup = one_hot(
+            depth, line * first_out, lambda r: r // rows_out * first_out + r % rows_out
+        )
+        g_mid[...] = mm_tn(regroup, total).astype(BF16).reshape(g_mid.shape)
+        for k in range(1, line):
+            zz = lax.rem(z + k, line)
+            copy(g_mid.at[zz], g_line.at[z], g_recv.at[quad + z], (me_d, zz * quad + q))
+        g_line[z] = g_mid[z]
+
     w_in, w_out = weights(w_buf, low_in, high_in), weights(o_buf, low_out, high_out)
-    spread_in, spread_out = spreads(
-        rows_in - low_in, high_in - low_in, rows_out - low_out, high_out - low_out
-    )
     result, _, saved = forward(
-        x_second.astype(F32), w_in, w_out, spread_in, spread_out, groups(lambda t: t // spots)
-    )
-    x1_ref[...] = (y1_ref[...].astype(F32) - result.astype(F32)).astype(BF16)
+        x_second.astype(F32), w_in, w_out, spread_in, spread_out, groups(lambda t: t // spots),
+        lambda: finish(2), sum_quad, lambda: finish(3),
+    )
+    out_ref[0] = (y1_ref[...].astype(F32) - result.astype(F32)).astype(BF16)
     back = backward(saved, d_first.astype(F32), w_in, w_out, spread_in, spread_out)
-    d2_ref[...] = (g2_ref[...].astype(F32) + back.astype(BF16).astype(F32)).astype(BF16)
-    exchanged(g_arrived, 2)
-    gw_ref[...] = jnp.sum(g_arrived[...].astype(F32), axis=0)[:rows_out]
+    out_ref[3] = (g2_ref[...].astype(F32) + back.astype(BF16).astype(F32)).astype(BF16)
+    for k in range(1, line):
+        zz = lax.rem(z + k, line)
+        await_into(g_line.at[zz], g_recv.at[quad + zz])
+    gw_ref[...] = jnp.sum(g_line[...].astype(F32), axis=0)[:rows_out]
     for made in pending:
         made.wait_send()
 
@@ -308,17 +346,19 @@
     line = n // quad
     slot = whole(2 * frames * spots // n)
     first_out = whole(rows_out)
-    grad_rows = n * first_out
+    depth = whole(line * rows_out)
     per_phase = line - 1 + 2 + 2 * (line - 1) + line + quad * (ndp - 1)
-    sends = 4 * per_phase + 3 * (n - 1) + ndp - 1
-    like = jax.ShapeDtypeStruct((tokens, width), BF16)
+    sends = 4 * per_phase + 2 * (n - 1) + ndp - 1 + quad - 1 + line - 1
     spec = pl.BlockSpec(memory_space=pltpu.VMEM)
     dma = pltpu.SemaphoreType.DMA
-    outs = pl.pallas_call(
+    stacked, grad = pl.pallas_call(
         functools.partial(block_kernel, n, ndp, frames, spots, rows_in, rows_out),
-        out_shape=(like,) * 4 + (jax.ShapeDtypeStruct((rows_out, columns_out), F32),),
+        out_shape=(
+            jax.ShapeDtypeStruct((4, tokens, width), BF16),
+            jax.ShapeDtypeStruct((rows_out, columns_out), F32),
+        ),
         in_specs=[spec] * 8,
-        out_specs=[spec] * 5,
+        out_specs=[spec] * 2,
         scratch_shapes=[
             pltpu.VMEM((ndp, line, quad, whole(2 * rows_in), columns_in), BF16),
             pltpu.VMEM((ndp, line, quad, whole(2 * rows_out), columns_out), BF16),
@@ -326,21 +366,24 @@
             pltpu.VMEM((n, slot, width), BF16),
             pltpu.VMEM((n, slot, width), BF16),
             pltpu.VMEM((n, slot, width), BF16),
-            pltpu.VMEM((ndp, grad_rows, columns_out), BF16),
-            pltpu.VMEM((ndp, grad_rows, columns_out), BF16),
-            pltpu.VMEM((n, first_out, columns_out), BF16),
-            pltpu.VMEM((n, first_out, columns_out), BF16),
+            pltpu.VMEM((ndp, quad, depth, columns_out), BF16),
+            pltpu.VMEM((ndp, quad, depth, columns_out), BF16),
+            pltpu.VMEM((quad, depth, columns_out), BF16),
+            pltpu.VMEM((quad, depth, columns_out), BF16),
+            pltpu.VMEM((line, first_out, columns_out), BF16),
+            pltpu.VMEM((line, first_out, columns_out), BF16),
             dma((4, line, quad)),
             dma((4, ndp, quad)),
-            dma((3, n)),
+            dma((2, n)),
             dma((ndp,)),
+            dma((quad + line,)),
             dma((sends,)),
         ],
         compiler_params=pltpu.CompilerParams(
             collective_id=0, has_side_effects=True, vmem_limit_bytes=60 * 2**20
         ),
     )(*[part.reshape(tokens, width) for part in operands[:4]], *operands[4:])
-    return tuple(part.reshape(shape) for part in outs[:4]) + (outs[4],)
+    return tuple(stacked[i].reshape(shape) for i in range(4)) + (grad,)
 
 
 def by_head(values, tokens):

time: 116 us -> 103 us (0.89)
  the two profiles are of different devices: /device:TPU:15 before, /device:TPU:0 now
where the time goes in v2:
time: 103 us
  Pallas kernels  99.5 us (97%)
  local copies, waits for them, and re-layouts  2.94 us (3%)
    pallas_call x1, Pallas kernels, body(): pl.pallas_call(functools.partial(block_kernel, n, ndp, frames, spots, row...  99.5 us
    slice x1, local copies, waits for them, and re-layouts, body(): return tuple((stacked[i].reshape(shape) for i in range(4))) + (grad,)  2.29 us

profile of v2, /device:TPU:0, one launch (start us, length us, event | category | flops | bytes accessed | tf_op | source)
XLA Modules:
  0.0 103.0 jit_solution(2040328425926499123)
XLA Ops:
  0.6 99.5 %shard_map.119 = (bf16[4,128,1152]{2,1,0:T(8,128)(2,1)}, f32[36,576]{1,0:T(8,128)}) custom-call(bf16[128,1152]{1,0:T(8,128)(2,1)} %bitcast.12, bf16[128,1152]{1,0:T(8,128)(2,1)} %bitcast.13, bf16[128,1152]{1,0:T(8,128)(2,1)} %bitcast.14, bf16[128,1152]{1,0:T(8,128)(2,1)} %bitcast.15, bf16[72,864]{1,0:T(8,128)(2,1)} %ws_ref.1, bf16[36,576]{1,0:T(8,128)(2,1)} %os_ref.1, ...), custom_call_target="tpu_custom_call" | custom-call | tf_op jit(solution)/shard_map/pallas_call | solution.py:354
  100.1 0.0 copy-start
  100.1 2.3 %fusion = (bf16[1,128,1152]{2,1,0:T(8,128)(2,1)}, bf16[1,128,1152]{2,1,0:T(8,128)(2,1)}, bf16[1,128,1152]{2,1,0:T(8,128)(2,1)}, bf16[1,128,1152]{2,1,0:T(8,128)(2,1)}) fusion(bf16[4,128,1152]{2,1,0:T(8,128)(2,1)} %get-tuple-element.7), kind=kLoop, calls=%fused_computation | loop fusion | bytes 2359296 | tf_op jit(solution)/shard_map/slice | solution.py:386
  102.4 0.0 copy-done
  102.4 0.6 copy.14
Async XLA Ops:
  100.1 2.3 %copy-start = (f32[36,576]{1,0:T(8,128)S(1)}, f32[36,576]{1,0:T(8,128)}, u32[]{:S(2)}) copy-start(f32[36,576]{1,0:T(8,128)} %get-tuple-element.22) | copy-start | bytes 248836

commit v3 on v2

--- a/solution.py
+++ b/solution.py
@@ -237,10 +237,10 @@
     spots_first, spots_second = piece(0), piece(1)
     packed = mm_tn(spots_first, y1_ref[...]) + mm_tn(spots_second, g2_ref[...])
     sent[...] = packed.astype(BF16).reshape(sent.shape)
+    spread_in, spread_out = spreads(0, first_in, 0, first_out)
+    spread_line(0)
     exchange(sent, arrived, 0)
     own_line(1)
-    spread_in, spread_out = spreads(0, first_in, 0, first_out)
-    spread_line(0)
     own_line(2)
     own_line(3)
     spread_far(0)
@@ -288,10 +288,6 @@
     for d in range(1, ndp):
         total = total + g_chip[d].astype(F32)
     g_sent[...] = total.astype(BF16)
-    for k in range(1, quad):
-        qq = lax.rem(q + k, quad)
-        copy(g_sent.at[qq], g_quad.at[q], g_recv.at[q], (me_d, z * quad + qq))
-    g_quad[q] = g_sent[q]
     low_in, low_out = rows_in // 16 * 16, rows_out // 16 * 16
     high_in, high_out = whole(2 * rows_in), whole(2 * rows_out)
     spread_in, spread_out = spreads(
@@ -305,6 +301,13 @@
     out_ref[1] = x_second
     d_first = (g1_ref[...].astype(F32) + mm(spots_second, rows)).astype(BF16)
     out_ref[2] = d_first
+
+    def send_quad():
+        finish(2)
+        for k in range(1, quad):
+            qq = lax.rem(q + k, quad)
+            copy(g_sent.at[qq], g_quad.at[q], g_recv.at[q], (me_d, z * quad + qq))
+        g_quad[q] = g_sent[q]
 
     def sum_quad():
         for k in range(1, quad):
@@ -323,8 +326,9 @@
     w_in, w_out = weights(w_buf, low_in, high_in), weights(o_buf, low_out, high_out)
     result, _, saved = forward(
         x_second.astype(F32), w_in, w_out, spread_in, spread_out, groups(lambda t: t // spots),
-        lambda: finish(2), sum_quad, lambda: finish(3),
-    )
+        send_quad, lambda: None, lambda: finish(3),
+    )
+    sum_quad()
     out_ref[0] = (y1_ref[...].astype(F32) - result.astype(F32)).astype(BF16)
     back = backward(saved, d_first.astype(F32), w_in, w_out, spread_in, spread_out)
     out_ref[3] = (g2_ref[...].astype(F32) + back.astype(BF16).astype(F32)).astype(BF16)

time: 103 us -> 106 us (1.029)
  Pallas kernels: 99.5 us -> 102 us
    pallas_call x1, Pallas kernels: 99.5 us -> 102 us  [body(): pl.pallas_call(functools.partial(block_kernel, n, ndp, frames, spots, row...]
where the time goes in v3:
time: 106 us
  Pallas kernels  102 us (96%)
  local copies, waits for them, and re-layouts  2.94 us (3%)
    pallas_call x1, Pallas kernels, body(): pl.pallas_call(functools.partial(block_kernel, n, ndp, frames, spots, row...  102 us
    slice x1, local copies, waits for them, and re-layouts, body(): return tuple((stacked[i].reshape(shape) for i in range(4))) + (grad,)  2.29 us

profile of v3, /device:TPU:0, one launch (start us, length us, event | category | flops | bytes accessed | tf_op | source)
XLA Modules:
  0.0 105.9 jit_solution(12665537128526936374)
XLA Ops:
  0.6 102.3 %shard_map.119 = (bf16[4,128,1152]{2,1,0:T(8,128)(2,1)}, f32[36,576]{1,0:T(8,128)}) custom-call(bf16[128,1152]{1,0:T(8,128)(2,1)} %bitcast.12, bf16[128,1152]{1,0:T(8,128)(2,1)} %bitcast.13, bf16[128,1152]{1,0:T(8,128)(2,1)} %bitcast.14, bf16[128,1152]{1,0:T(8,128)(2,1)} %bitcast.15, bf16[72,864]{1,0:T(8,128)(2,1)} %ws_ref.1, bf16[36,576]{1,0:T(8,128)(2,1)} %os_ref.1, ...), custom_call_target="tpu_custom_call" | custom-call | tf_op jit(solution)/shard_map/pallas_call | solution.py:358
  102.9 0.0 copy-start
  103.0 2.3 %fusion = (bf16[1,128,1152]{2,1,0:T(8,128)(2,1)}, bf16[1,128,1152]{2,1,0:T(8,128)(2,1)}, bf16[1,128,1152]{2,1,0:T(8,128)(2,1)}, bf16[1,128,1152]{2,1,0:T(8,128)(2,1)}) fusion(bf16[4,128,1152]{2,1,0:T(8,128)(2,1)} %get-tuple-element.7), kind=kLoop, calls=%fused_computation | loop fusion | bytes 2359296 | tf_op jit(solution)/shard_map/slice | solution.py:390
  105.2 0.0 copy-done
  105.3 0.6 copy.14
Async XLA Ops:
  102.9 2.3 %copy-start = (f32[36,576]{1,0:T(8,128)S(1)}, f32[36,576]{1,0:T(8,128)}, u32[]{:S(2)}) copy-start(f32[36,576]{1,0:T(8,128)} %get-tuple-element.22) | copy-start | bytes 248836

commit v4 on v2

--- a/solution.py
+++ b/solution.py
@@ -255,19 +255,19 @@
     def next_phases():
         spread_far(1)
         own_sides(2)
-        spread_line(2)
         own_sides(3)
-        spread_line(3)
 
     w_in, w_out = weights(w_buf, 0, first_in), weights(o_buf, 0, first_out)
     result, mixed, saved = forward(
         mm(take_first, rows), w_in, w_out, spread_in, spread_out, groups(lambda r: r % per),
         lambda: finish(0), next_phases, lambda: finish(1),
     )
+    spread_line(2)
     back = backward(saved, cotangent, w_in, w_out, spread_in, spread_out).astype(BF16)
     packed = mm_tn(take_first, result) + mm_tn(take_second, back)
     answer[...] = packed.astype(BF16).reshape(answer.shape)
     exchange(answer, returned, 1)
+    spread_line(3)
 
     depth = g_sent.shape[1]
     by_quad = one_hot(

time: 103 us -> 104 us (level)
  Pallas kernels: 99.5 us -> 101 us
    pallas_call x1, Pallas kernels: 99.5 us -> 101 us  [body(): pl.pallas_call(functools.partial(block_kernel, n, ndp, frames, spots, row...]
where the time goes in v4:
time: 104 us
  Pallas kernels  101 us (97%)
  local copies, waits for them, and re-layouts  2.94 us (3%)
    pallas_call x1, Pallas kernels, body(): pl.pallas_call(functools.partial(block_kernel, n, ndp, frames, spots, row...  101 us
    slice x1, local copies, waits for them, and re-layouts, body(): return tuple((stacked[i].reshape(shape) for i in range(4))) + (grad,)  2.29 us

profile of v4, /device:TPU:0, one launch (start us, length us, event | category | flops | bytes accessed | tf_op | source)
XLA Modules:
  0.0 104.2 jit_solution(17677574708464442826)
XLA Ops:
  0.6 100.6 %shard_map.119 = (bf16[4,128,1152]{2,1,0:T(8,128)(2,1)}, f32[36,576]{1,0:T(8,128)}) custom-call(bf16[128,1152]{1,0:T(8,128)(2,1)} %bitcast.12, bf16[128,1152]{1,0:T(8,128)(2,1)} %bitcast.13, bf16[128,1152]{1,0:T(8,128)(2,1)} %bitcast.14, bf16[128,1152]{1,0:T(8,128)(2,1)} %bitcast.15, bf16[72,864]{1,0:T(8,128)(2,1)} %ws_ref.1, bf16[36,576]{1,0:T(8,128)(2,1)} %os_ref.1, ...), custom_call_target="tpu_custom_call" | custom-call | tf_op jit(solution)/shard_map/pallas_call | solution.py:354
  101.2 0.0 copy-start
  101.2 2.3 %fusion = (bf16[1,128,1152]{2,1,0:T(8,128)(2,1)}, bf16[1,128,1152]{2,1,0:T(8,128)(2,1)}, bf16[1,128,1152]{2,1,0:T(8,128)(2,1)}, bf16[1,128,1152]{2,1,0:T(8,128)(2,1)}) fusion(bf16[4,128,1152]{2,1,0:T(8,128)(2,1)} %get-tuple-element.7), kind=kLoop, calls=%fused_computation | loop fusion | bytes 2359296 | tf_op jit(solution)/shard_map/slice | solution.py:386
  103.5 0.0 copy-done
  103.5 0.6 copy.14
Async XLA Ops:
  101.2 2.3 %copy-start = (f32[36,576]{1,0:T(8,128)S(1)}, f32[36,576]{1,0:T(8,128)}, u32[]{:S(2)}) copy-start(f32[36,576]{1,0:T(8,128)} %get-tuple-element.22) | copy-start | bytes 248836
